TPU v7x, 128 devices: a whole 4x4x4 slice. The times are simulated.
128 devices in a mesh: grp: 4 (over y), dev: 32 (over x, z, core).
Axes of the slice: x: 4, y: 4, z: 4, core: 2. Of those that a mesh axis runs over, the one named last changes fastest.
Arguments:
- panel_nodes: float32 [3, 1048576], P(None, ('grp', 'dev')), may hold values from -1.6 to 1.6, as said below
- density: float32 [1048576], P(('grp', 'dev')), may hold values from -6 to 6
- crevice_routes: int32 [65536, 2], P(('grp', 'dev')), may hold values from 0 to 127, all different within a row; in each aligned block of 512 rows (0 to 511, 512 to 1023, ...) at most 16 rows name the same one
- crevice_centre: int32 [65536, 2], P(('grp', 'dev')), may hold values from 0 to 511
- centres: float32 [3, 65536], P(None, ('grp', 'dev')), may hold values from -0.3 to 0.3, as said below
- targets: float32 [3, 1048576], P(None, ('grp', 'dev')), may hold values from -0.8 to 0.8, as said below
- centre_home: int32 [65536, 1], P(('grp', 'dev')), may hold values from 0 to 127; in each aligned block of 512 rows (0 to 511, 512 to 1023, ...) at most 8 rows name the same one
- upsample: float32 [64, 16], replicated, may hold values from 0 to 1, as said below
- fine_weights: float32 [64], replicated, may hold values from 0.005 to 0.05
Outputs:
- returned: float32 [2097152], P(('grp', 'dev'))
Inputs may be any that keep to these rules, and one draw needn't show every extreme that they name: `crevice_routes`: each device's 512 panels name at most 16 (panel, route) pairs for any one owner device, and some owner reaches 16 in every draw; the 2 owners of one panel differ. `centre_home`: among the 512 centres of one device at most 8 have the same home, and that bound is reached in every draw; entries of returned with no centre are zero. `panel_nodes`: every point in the convex hull of one panel's nodes lies at distance 0.9 or more from the anchor; every panel node lies within 1.6 of the anchor. `centres`: every centre lies within 0.3 of the anchor. `targets`: each target node lies at distance 0.3 to 0.5 from its centre. `upsample`: entries are positive and each row sums to one.
All inputs are finite; a program needn't handle non-finite values.
Results may differ from a plain program's by a relative error of at most 0.0003.
Values sent between devices are 32-bit elements; how exact they have to be, the bound alone decides.
A program may use at most 64 MiB of HBM per device.

v0:
```python
import math

import jax
import jax.numpy as jnp
from jax import lax
from jax.sharding import PartitionSpec as P

ORDER = 8


def route_rank(destination, count):
    onehot = (destination[:, None] == jnp.arange(count, dtype=jnp.int32)[None, :]).astype(jnp.int32)
    before = jnp.cumsum(onehot, axis=0) - onehot
    return jnp.sum(before * onehot, axis=1)


def refine(coarse_all, upsample, fine_weights):
    upper = jnp.einsum("sck,nk->scn", coarse_all, upsample, precision=lax.Precision.HIGHEST)
    strength = upper[:, 3, :] * fine_weights[None, :]
    return jnp.concatenate([upper[:, :3, :], strength[:, None, :]], axis=1)


def expansion_terms(sources, centre_pos, target_pos):
    src_vec = sources[:, :3, :] - centre_pos[:, :, None]
    tgt_vec = target_pos - centre_pos[:, :, None]
    src_dist = jnp.sqrt(jnp.sum(src_vec * src_vec, axis=1))
    tgt_dist = jnp.sqrt(jnp.sum(tgt_vec * tgt_vec, axis=1))
    inner = jnp.sum(src_vec[:, :, :, None] * tgt_vec[:, :, None, :], axis=1)
    cosine = inner / (src_dist[:, :, None] * tgt_dist[:, None, :])
    ratio = tgt_dist[:, None, :] / src_dist[:, :, None]
    p_prev = jnp.ones_like(cosine)
    p_now = cosine
    power = ratio
    total = 1.0 + ratio * cosine
    for level in range(1, ORDER):
        p_next = ((2 * level + 1) * cosine * p_now - level * p_prev) / (level + 1)
        power = power * ratio
        total = total + power * p_next
        p_prev, p_now = (p_now, p_next)
    kernel = total / src_dist[:, :, None]
    return jnp.sum(sources[:, 3, :, None] * kernel, axis=1)


def per_device(
    panel_nodes,
    density,
    crevice_routes,
    crevice_centre,
    centres,
    targets,
    centre_home,
    upsample,
    fine_weights,
):
    devices = lax.axis_size(("grp", "dev"))
    panels = crevice_routes.shape[0]
    fanout = crevice_routes.shape[1]
    centre_count = centres.shape[1]
    capacity = max(2, 2 * panels * fanout // devices)
    capacity_back = max(2, 2 * centre_count // devices)
    nodes = upsample.shape[1]
    coarse_all = jnp.concatenate(
        [
            panel_nodes.reshape(3, panels, nodes).transpose(1, 0, 2),
            density.reshape(panels, 1, nodes),
        ],
        axis=1,
    )
    payload = refine(coarse_all, upsample, fine_weights)
    per_row = payload.shape[2]
    payload = payload.reshape(panels, 4 * per_row)
    destination = crevice_routes.reshape(-1)
    slot_index = destination * capacity + route_rank(destination, devices)
    filler = jnp.concatenate(
        [jnp.full((3 * per_row,), 2.0, jnp.float32), jnp.zeros((per_row,), jnp.float32)]
    )
    slots = devices * capacity
    outgoing = (
        jnp.broadcast_to(filler[None, :], (slots, 4 * per_row))
        .at[slot_index]
        .set(jnp.repeat(payload, fanout, axis=0))
    )
    centre_slot = (
        jnp.full((slots,), float(centre_count), jnp.float32)
        .at[slot_index]
        .set(crevice_centre.reshape(-1).astype(jnp.float32))
    )
    incoming, incoming_ids = (
        lax.all_to_all(outgoing, ("grp", "dev"), split_axis=0, concat_axis=0, tiled=True),
        lax.all_to_all(centre_slot, ("grp", "dev"), split_axis=0, concat_axis=0, tiled=True),
    )
    incoming = incoming.reshape(slots, 4, per_row)
    centre_ids = incoming_ids.astype(jnp.int32)
    target_all = targets.reshape(3, centre_count, nodes)
    block = math.gcd(slots, 512)

    def one_block(pieces):
        sources, ids = pieces
        safe_ids = jnp.minimum(ids, centre_count - 1)
        centre_pos = centres[:, safe_ids].T
        target_pos = target_all[:, safe_ids, :].transpose(1, 0, 2)
        return expansion_terms(sources, centre_pos, target_pos)

    terms = lax.map(
        one_block,
        (
            incoming.reshape(slots // block, block, 4, incoming.shape[2]),
            centre_ids.reshape(slots // block, block),
        ),
    )
    potential = jax.ops.segment_sum(
        terms.reshape(slots, nodes), centre_ids, num_segments=centre_count + 1
    )[:centre_count]
    home = centre_home.reshape(-1)
    back_index = home * capacity_back + route_rank(home, devices)
    sending = jnp.zeros((devices * capacity_back, nodes), jnp.float32).at[back_index].set(potential)
    returned = lax.all_to_all(sending, ("grp", "dev"), split_axis=0, concat_axis=0, tiled=True)
    return returned.reshape(-1)


def solution(mesh):
    placed = (
        P(None, ("grp", "dev")),
        P(("grp", "dev")),
        P(("grp", "dev"), None),
        P(("grp", "dev"), None),
        P(None, ("grp", "dev")),
        P(None, ("grp", "dev")),
        P(("grp", "dev"), None),
        P(),
        P(),
    )
    return jax.shard_map(
        per_device, mesh=mesh, in_specs=placed, out_specs=P(("grp", "dev")), check_vma=False
    )
```

profile of v0, /device:TPU:1, one launch (start us, length us, event | category | flops | bytes accessed | tf_op | source)
XLA Modules:
  0.0 163.7 jit_solution(7936346815332251436)
XLA Ops:
  3.5 4.3 %scatter_custom_fusion = f32[2048]{0:T(1024)S(1)} fusion(s32[1024]{0:T(1024)S(1)} %bitcast.68, f32[1024]{0:T(1024)S(1)} %reshape.180, f32[]{:T(128)} %constant.169.clone.1), kind=kCustom, calls=%fused_computation.73 | custom fusion | bytes 8196 | tf_op jit(solution)/shard_map/scatter | solution.py:86
  8.5 11.5 %all-to-all-start = ((f32[128,16,1]{1,2,0:T(1,128)}), f32[128,16,1]{1,2,0:T(1,128)S(1)}, u32[]{:S(2)}, u32[]{:S(2)}) async-start(f32[128,16,1]{1,2,0:T(1,128)} %bitcast.17), calls=%async_computation | async-start | bytes 131072 | tf_op jit(solution)/shard_map/all_to_all | solution.py:90
  23.0 1.5 broadcast_in_dim.22
  24.4 7.7 %scatter_fusion = f32[2048,256]{1,0:T(8,128)} fusion(f32[2048,256]{1,0:T(8,128)} %broadcast_in_dim.22, s32[1024]{0:T(1024)S(1)} %bitcast.69, f32[1024,256]{1,0:T(8,128)S(1)} %reshape.188), kind=kCustom, calls=%fused_computation.3 | custom fusion | bytes 3149824 | tf_op jit(solution)/shard_map/scatter | solution.py:81
  32.1 9.8 %all-to-all-start.1 = ((f32[128,16,256]{2,1,0:T(8,128)}), f32[128,16,256]{2,1,0:T(8,128)S(1)}, u32[]{:S(2)}, u32[]{:S(2)}) async-start(f32[128,16,256]{2,1,0:T(8,128)} %bitcast.21), calls=%async_computation.1 | async-start | bytes 4194304 | tf_op jit(solution)/shard_map/all_to_all | solution.py:89
  42.4 1.2 reshape.157
  43.6 1.5 copy.115
  45.9 26.2 %all-to-all-done.1 = f32[128,16,256]{2,1,0:T(8,128)S(1)} async-done(((f32[128,16,256]{2,1,0:T(8,128)}), f32[128,16,256]{2,1,0:T(8,128)S(1)}, u32[]{:S(2)}, u32[]{:S(2)}) %all-to-all-start.1) | async-done | bytes 2097184 | tf_op jit(solution)/shard_map/all_to_all | solution.py:89
  72.1 3.1 %reshape_reshape.3 = f32[4,512,4,64]{3,2,1,0:T(4,128)} reshape(f32[128,16,256]{2,1,0:T(8,128)S(1)} %all-to-all-done.1) | data formatting | bytes 4194304 | tf_op jit(solution)/shard_map/reshape;reshape | solution.py:107
  75.2 4.8 %copy.114 = f32[4,512,4,64]{1,3,2,0:T(8,128)} copy(f32[4,512,4,64]{3,2,1,0:T(4,128)} %reshape_reshape.3) | data formatting | bytes 4194304 | tf_op jit(solution)/shard_map/while | solution.py:104
  80.0 53.7 %while.12 = (s32[]{:T(128)}, f32[4,512,16]{1,2,0:T(8,128)S(1)}, f32[4,512,4,64]{1,3,2,0:T(8,128)}, s32[4,512]{1,0:T(4,128)S(1)}, f32[3,512,16]{2,0,1:T(4,128)}, /*index=5*/f32[3,512]{0,1:T(8,128)S(1)}, s32[]{:T(128)}) while((s32[]{:T(128)}, f32[4,512,16]{1,2,0:T(8,128)S(1)}, f32[4,512,4,64]{1,3,2,0:T(8,128)}, s32[4,512]{1,0:T(4,128)S(1)}, ...), condition=%wide.region_13.14_spmd, body=%wide.region_8.13_spmd.sunk | while | flops 35974144 | bytes 8374369 | solution.py:104
  80.1 2.7 %gather_fusion = f32[512,3,16]{2,1,0:T(4,128)S(1)} fusion(f32[3,512,16]{2,0,1:T(4,128)} %get-tuple-element.209, s32[1024]{0:T(1024)S(1)} %pad_clamp_fusion.2), kind=kCustom, calls=%fused_computation.clone.1 | custom fusion | bytes 198656 | tf_op jit(solution)/shard_map/while/body/eval_jaxpr/gather | solution.py:101
  82.8 1.0 gather_fusion.1
  83.8 2.8 %multiply_reduce_fusion.8 = (f32[512,16]{1,0:T(8,128)S(1)}, f32[512,3,16]{2,1,0:T(4,128)S(1)}) fusion(f32[512,3,16]{2,1,0:T(4,128)S(1)} %gather_fusion, f32[512,3]{1,0:T(8,128)S(1)} %gather_fusion.1), kind=kLoop, calls=%fused_computation.31.clone.1 | loop fusion | flops 65536 | bytes 235520 | tf_op jit(solution)/shard_map/while/body/eval_jaxpr/reduce_sum | solution.py:27
  87.1 1.1 dynamic-slice_bitcast_fusion.2
  89.0 4.4 %multiply_reduce_fusion.11 = f32[512,16]{0,1:T(8,128)S(1)} fusion(f32[512,64,16]{0,2,1:T(8,128)S(1)} %multiply_reduce_fusion.10, f32[512,64]{0,1:T(8,128)S(1)} %sqrt.22, f32[512,16]{0,1:T(8,128)S(1)} %sqrt.23, f32[512,64]{0,1:T(8,128)S(1)} %slice_bitcast_fusion.4), kind=kLoop, calls=%fused_computation.30.clone.1 | loop fusion | flops 33021952 | bytes 2424832 | tf_op jit(solution)/shard_map/while/body/eval_jaxpr/reduce_sum | solution.py:41
  93.5 2.7 %gather_fusion = f32[512,3,16]{2,1,0:T(4,128)S(1)} fusion(f32[3,512,16]{2,0,1:T(4,128)} %get-tuple-element.209, s32[1024]{0:T(1024)S(1)} %pad_clamp_fusion.2), kind=kCustom, calls=%fused_computation.clone.1 | custom fusion | bytes 198656 | tf_op jit(solution)/shard_map/while/body/eval_jaxpr/gather | solution.py:101
  97.3 2.8 %multiply_reduce_fusion.8 = (f32[512,16]{1,0:T(8,128)S(1)}, f32[512,3,16]{2,1,0:T(4,128)S(1)}) fusion(f32[512,3,16]{2,1,0:T(4,128)S(1)} %gather_fusion, f32[512,3]{1,0:T(8,128)S(1)} %gather_fusion.1), kind=kLoop, calls=%fused_computation.31.clone.1 | loop fusion | flops 65536 | bytes 235520 | tf_op jit(solution)/shard_map/while/body/eval_jaxpr/reduce_sum | solution.py:27
  100.5 1.1 dynamic-slice_bitcast_fusion.2
  102.4 4.4 %multiply_reduce_fusion.11 = f32[512,16]{0,1:T(8,128)S(1)} fusion(f32[512,64,16]{0,2,1:T(8,128)S(1)} %multiply_reduce_fusion.10, f32[512,64]{0,1:T(8,128)S(1)} %sqrt.22, f32[512,16]{0,1:T(8,128)S(1)} %sqrt.23, f32[512,64]{0,1:T(8,128)S(1)} %slice_bitcast_fusion.4), kind=kLoop, calls=%fused_computation.30.clone.1 | loop fusion | flops 33021952 | bytes 2424832 | tf_op jit(solution)/shard_map/while/body/eval_jaxpr/reduce_sum | solution.py:41
  106.9 2.7 %gather_fusion = f32[512,3,16]{2,1,0:T(4,128)S(1)} fusion(f32[3,512,16]{2,0,1:T(4,128)} %get-tuple-element.209, s32[1024]{0:T(1024)S(1)} %pad_clamp_fusion.2), kind=kCustom, calls=%fused_computation.clone.1 | custom fusion | bytes 198656 | tf_op jit(solution)/shard_map/while/body/eval_jaxpr/gather | solution.py:101
  109.7 1.0 gather_fusion.1
  110.7 2.8 %multiply_reduce_fusion.8 = (f32[512,16]{1,0:T(8,128)S(1)}, f32[512,3,16]{2,1,0:T(4,128)S(1)}) fusion(f32[512,3,16]{2,1,0:T(4,128)S(1)} %gather_fusion, f32[512,3]{1,0:T(8,128)S(1)} %gather_fusion.1), kind=kLoop, calls=%fused_computation.31.clone.1 | loop fusion | flops 65536 | bytes 235520 | tf_op jit(solution)/shard_map/while/body/eval_jaxpr/reduce_sum | solution.py:27
  113.9 1.1 dynamic-slice_bitcast_fusion.2
  115.9 4.4 %multiply_reduce_fusion.11 = f32[512,16]{0,1:T(8,128)S(1)} fusion(f32[512,64,16]{0,2,1:T(8,128)S(1)} %multiply_reduce_fusion.10, f32[512,64]{0,1:T(8,128)S(1)} %sqrt.22, f32[512,16]{0,1:T(8,128)S(1)} %sqrt.23, f32[512,64]{0,1:T(8,128)S(1)} %slice_bitcast_fusion.4), kind=kLoop, calls=%fused_computation.30.clone.1 | loop fusion | flops 33021952 | bytes 2424832 | tf_op jit(solution)/shard_map/while/body/eval_jaxpr/reduce_sum | solution.py:41
  120.4 2.7 %gather_fusion = f32[512,3,16]{2,1,0:T(4,128)S(1)} fusion(f32[3,512,16]{2,0,1:T(4,128)} %get-tuple-element.209, s32[1024]{0:T(1024)S(1)} %pad_clamp_fusion.2), kind=kCustom, calls=%fused_computation.clone.1 | custom fusion | bytes 198656 | tf_op jit(solution)/shard_map/while/body/eval_jaxpr/gather | solution.py:101
  124.2 2.8 %multiply_reduce_fusion.8 = (f32[512,16]{1,0:T(8,128)S(1)}, f32[512,3,16]{2,1,0:T(4,128)S(1)}) fusion(f32[512,3,16]{2,1,0:T(4,128)S(1)} %gather_fusion, f32[512,3]{1,0:T(8,128)S(1)} %gather_fusion.1), kind=kLoop, calls=%fused_computation.31.clone.1 | loop fusion | flops 65536 | bytes 235520 | tf_op jit(solution)/shard_map/while/body/eval_jaxpr/reduce_sum | solution.py:27
  127.4 1.1 dynamic-slice_bitcast_fusion.2
  129.3 4.4 %multiply_reduce_fusion.11 = f32[512,16]{0,1:T(8,128)S(1)} fusion(f32[512,64,16]{0,2,1:T(8,128)S(1)} %multiply_reduce_fusion.10, f32[512,64]{0,1:T(8,128)S(1)} %sqrt.22, f32[512,16]{0,1:T(8,128)S(1)} %sqrt.23, f32[512,64]{0,1:T(8,128)S(1)} %slice_bitcast_fusion.4), kind=kLoop, calls=%fused_computation.30.clone.1 | loop fusion | flops 33021952 | bytes 2424832 | tf_op jit(solution)/shard_map/while/body/eval_jaxpr/reduce_sum | solution.py:41
  134.1 11.5 %scatter_custom_fusion.2 = f32[513,16]{1,0:T(8,128)S(1)} fusion(s32[2048]{0:T(1024)S(1)} %reshape.194, f32[2048,16]{1,0:T(8,128)S(1)} %bitcast.61, f32[]{:T(128)} %constant.165.clone.1), kind=kCustom, calls=%fused_computation.60 | custom fusion | flops 32768 | bytes 32836 | tf_op jit(solution)/shard_map/scatter-add | solution.py:111
  145.6 1.9 %scatter_custom_fusion.3 = f32[1024,16]{1,0:T(8,128)S(1)} fusion(s32[512]{0:T(512)S(1)} %bitcast.73, f32[513,16]{1,0:T(8,128)S(1)} %scatter_custom_fusion.2, f32[]{:T(128)} %constant.165.clone.1), kind=kCustom, calls=%fused_computation.48 | custom fusion | bytes 327684 | tf_op jit(solution)/shard_map/scatter | solution.py:116
  147.7 13.7 %all_to_all.27 = f32[128,1,128]{2,1,0:T(1,128)S(1)} all-to-all(f32[128,1,128]{2,1,0:T(1,128)S(1)} %reshape.226), channel_id=1, replica_groups=mesh['grp'=4,'dev'=32] {'grp','dev'}, dimensions={0} | all-to-all | bytes 131072 | tf_op jit(solution)/shard_map/all_to_all | solution.py:117
  (117 shorter events, 17.9 us)
Async XLA Ops:
  0.0 20.8 %copy-start = (f32[64,16]{0,1:T(8,128)S(1)}, f32[64,16]{0,1:T(8,128)}, u32[]{:S(2)}) copy-start(f32[64,16]{0,1:T(8,128)} %param.18) | copy-start | bytes 12292
  0.0 2.8 %copy-start.6 = (s32[512,2]{0,1:T(2,128)S(1)}, s32[512,2]{0,1:T(2,128)}, u32[]{:S(2)}) copy-start(s32[512,2]{0,1:T(2,128)} %param.14) | copy-start | bytes 12292
  2.2 17.8 %copy-start.3 = (f32[8192]{0:T(1024)S(1)}, f32[8192]{0:T(1024)}, u32[]{:S(2)}) copy-start(f32[8192]{0:T(1024)} %param.12) | copy-start | bytes 98308
  2.6 17.7 %copy-start.1 = (f32[3,8192]{1,0:T(4,128)S(1)}, f32[3,8192]{1,0:T(4,128)}, u32[]{:S(2)}) copy-start(f32[3,8192]{1,0:T(4,128)} %param.11) | copy-start | bytes 294916
  3.5 18.0 %copy-start.8 = (f32[64]{0:T(128)S(1)}, f32[64]{0:T(128)}, u32[]{:S(2)}) copy-start(f32[64]{0:T(128)} %param.19) | copy-start | bytes 772
  8.5 23.6 %all-to-all-start = ((f32[128,16,1]{1,2,0:T(1,128)}), f32[128,16,1]{1,2,0:T(1,128)S(1)}, u32[]{:S(2)}, u32[]{:S(2)}) async-start(f32[128,16,1]{1,2,0:T(1,128)} %bitcast.17), calls=%async_computation | async-start | bytes 131072 | tf_op jit(solution)/shard_map/all_to_all | solution.py:90
  21.8 1.1 copy-start.7
  32.1 9.8 %copy-start.4 = (s32[512,1]{0,1:T(1,128)S(1)}, s32[512,1]{0,1:T(1,128)}, u32[]{:S(2)}) copy-start(s32[512,1]{0,1:T(1,128)} %param.17) | copy-start | bytes 6148
  32.1 40.0 %all-to-all-start.1 = ((f32[128,16,256]{2,1,0:T(8,128)}), f32[128,16,256]{2,1,0:T(8,128)S(1)}, u32[]{:S(2)}, u32[]{:S(2)}) async-start(f32[128,16,256]{2,1,0:T(8,128)} %bitcast.21), calls=%async_computation.1 | async-start | bytes 4194304 | tf_op jit(solution)/shard_map/all_to_all | solution.py:89
  41.9 3.2 %copy-start.5 = (f32[3,512]{1,0:T(4,128)S(1)}, f32[3,512]{1,0:T(4,128)}, u32[]{:S(2)}) copy-start(f32[3,512]{1,0:T(4,128)} %param.15) | copy-start | bytes 18436
  75.2 4.8 %copy-start.2 = (f32[4,512,16]{1,2,0:T(8,128)S(1)}, f32[4,512,16]{1,2,0:T(8,128)}, u32[]{:S(2)}) copy-start(f32[4,512,16]{1,2,0:T(8,128)} %custom-call.4) | copy-start | bytes 393220
where the time goes:
time: 165 us; the launch traced here: 164 us
  local copies, waits for them, and re-layouts  55 us (33%)
  other arithmetic  46.2 us (28%)
  waiting for transfers between devices  26.2 us (16%)
  starting transfers between devices  21.3 us (13%)
  blocking collectives  13.7 us (8%)
    all_to_all x1, waiting for transfers between devices, per_device(): lax.all_to_all(outgoing, ('grp', 'dev'), split_axis=0, concat_axis=0, til...  26.2 us
    reduce_sum x4, other arithmetic, expansion_terms(): return jnp.sum(sources[:, 3, :, None] * kernel, axis=1)  17.8 us
    all_to_all x1, blocking collectives, per_device(): lax.all_to_all(sending, ('grp', 'dev'), split_axis=0, concat_axis=0, tile...  13.7 us
    scatter-add x1, other arithmetic, per_device(): jax.ops.segment_sum(terms.reshape(slots, nodes), centre_ids, num_segments...  11.5 us
    all_to_all x1, starting transfers between devices, per_device(): lax.all_to_all(centre_slot, ('grp', 'dev'), split_axis=0, concat_axis=0,...  11.5 us
    reduce_sum x4, other arithmetic, expansion_terms(): tgt_dist = jnp.sqrt(jnp.sum(tgt_vec * tgt_vec, axis=1))  11.3 us
    gather x4, local copies, waits for them, and re-layouts, one_block(): target_pos = target_all[:, safe_ids, :].transpose(1, 0, 2)  10.9 us
    all_to_all x1, starting transfers between devices, per_device(): lax.all_to_all(outgoing, ('grp', 'dev'), split_axis=0, concat_axis=0, til...  9.77 us
  transfers between devices with their start and end apart: 2, of which 1 were waited for; matrix products, arithmetic and copies ran while one was open for 10% of the time, Pallas kernels for 0%

commit v1 on v0

v1 whole, which is shorter than its diff:
```python
import functools
import math

import jax
import jax.numpy as jnp
from jax import lax
from jax.experimental import pallas as pl
from jax.experimental.pallas import tpu as pltpu
from jax.sharding import PartitionSpec as P

MESH = pl.DeviceIdType.MESH
F32, BF16 = jnp.float32, jnp.bfloat16
ORDER = 8
NODES = 16
FINE = 64
NN = (((1,), (0,)), ((), ()))
NT = (((1,), (1,)), ((), ()))
TERMS = [(m, l) for m in range(ORDER + 1) for l in range(m, ORDER + 1)]
ROWS = 88


def rows_of():
    at, place = {}, 0
    for m in range(ORDER + 1):
        for l in range(m, ORDER + 1):
            for part in range(1 if m == 0 else 2):
                at[(m, l, part)] = place
                place += 1
    return at


PLACE = rows_of()


def weight(l, m):
    lead = math.factorial(2 * l) / (2**l * math.factorial(l) * math.factorial(l - m))
    return (1 if m == 0 else 2) * math.factorial(l - m) / math.factorial(l + m) * lead * lead


def harmonics(x, y, z, sq, start, emit):
    re, im = start, None
    for m in range(ORDER + 1):
        if m == 1:
            re, im = x * start, y * start
        elif m > 1:
            re, im = x * re - y * im, x * im + y * re
        old_re = old_im = None
        now_re, now_im = re, im
        for l in range(m, ORDER + 1):
            emit(m, l, 0, now_re)
            if m:
                emit(m, l, 1, now_im)
            if l == ORDER:
                break
            next_re = z * now_re
            next_im = z * now_im if m else None
            if l > m:
                damp = sq * ((l * l - m * m) / (4.0 * l * l - 1.0))
                next_re = next_re - damp * old_re
                if m:
                    next_im = next_im - damp * old_im
            old_re, old_im, now_re, now_im = now_re, now_im, next_re, next_im


def split3(value):
    hi = value.astype(BF16)
    rest = value - hi.astype(F32)
    mid = rest.astype(BF16)
    return hi, mid, (rest - mid.astype(F32)).astype(BF16)


def dot(a, b, dims=NN):
    return lax.dot_general(a, b, dims, preferred_element_type=F32)


def iota(shape, axis):
    return lax.broadcasted_iota(jnp.int32, shape, axis)


def kernel(
    grp_size,
    dev_size,
    pay_ref,
    routes_ref,
    ids_ref,
    home_ref,
    centres_ref,
    targets_ref,
    up_ref,
    fw_ref,
    out_ref,
    rank_scr,
    value_scr,
    out_box,
    in_box,
    back_box,
    table,
    pick_back,
    moments,
    local,
    send_sem,
    recv_sem,
    back_send_sem,
    back_recv_sem,
):
    n = grp_size * dev_size
    panels = pay_ref.shape[0]
    count = centres_ref.shape[1]
    groups = n // 8
    me = lax.axis_index("grp") * dev_size + lax.axis_index("dev")

    def device(p):
        return (p // dev_size, p % dev_size)

    barrier = pltpu.get_barrier_semaphore()

    def greet(i, carry):
        pl.semaphore_signal(barrier, inc=1, device_id=device((me + i) % n), device_id_type=MESH)
        return carry

    lax.fori_loop(1, n, greet, 0)

    owner = iota((n, panels), 0)
    first, second = owner == routes_ref[0:1, :], owner == routes_ref[1:2, :]
    named = first | second
    earlier = (iota((panels, panels), 0) < iota((panels, panels), 1)).astype(F32).astype(BF16)
    rank = dot(named.astype(F32).astype(BF16), earlier)
    rank_scr[...] = jnp.where(named, rank, -1.0)
    ids = ids_ref[...].astype(F32) - 256.0
    value_scr[...] = jnp.where(first, ids[0:1, :], jnp.where(second, ids[1:2, :], 0.0))
    pay = pay_ref[...]
    parts = jnp.concatenate(split3(jnp.concatenate([pay, pay], axis=1)), axis=1)
    ones = jnp.ones((panels, 128), BF16)
    block = 16
    left = iota((block * 8, 128), 1) < 64
    own_row = iota((block * 8, 128), 1) % 8 == iota((block * 8, 128), 0) % 8
    row8 = iota((8, panels), 0).astype(F32)

    def build(step, carry):
        base = step * block
        low, high, low_id, high_id = [], [], [], []
        for d in range(block):
            slot = jnp.broadcast_to(rank_scr[pl.ds(base + d, 1), :], (8, panels))
            value = jnp.broadcast_to(value_scr[pl.ds(base + d, 1), :], (8, panels))
            is_low, is_high = slot == row8, slot == row8 + 8.0
            low.append(jnp.where(is_low, 1.0, 0.0))
            high.append(jnp.where(is_high, 1.0, 0.0))
            low_id.append(jnp.where(is_low, value, 0.0))
            high_id.append(jnp.where(is_high, value, 0.0))

        def gather(pieces, what):
            return dot(jnp.concatenate(pieces, axis=0).astype(BF16), what)

        a, b = gather(low, parts), gather(high, parts)
        a = a[:, 0:128] + a[:, 128:256] + a[:, 256:384]
        b = b[:, 0:128] + b[:, 128:256] + b[:, 256:384]
        out_box[pl.ds(base, block), 0:8, :] = jnp.where(left, a, b).reshape(block, 8, 128)
        named_id = jnp.where(left, gather(low_id, ones), gather(high_id, ones)) + 256.0
        named_id = jnp.where(own_row, named_id, 0.0).reshape(block, 8, 128)
        out_box[pl.ds(base, block), 8, :] = jnp.sum(named_id, axis=1)
        return carry

    lax.fori_loop(0, n // block, build, 0)

    pl.semaphore_wait(barrier, n - 1)

    def send(i, carry):
        p = (me + i) % n
        pltpu.make_async_remote_copy(
            src_ref=out_box.at[p],
            dst_ref=in_box.at[me],
            send_sem=send_sem,
            recv_sem=recv_sem.at[me // 8],
            device_id=device(p),
            device_id_type=MESH,
        ).start()
        return carry

    lax.fori_loop(1, n, send, 0)
    pltpu.make_async_copy(out_box.at[me], in_box.at[me], recv_sem.at[me // 8]).start()

    home = iota((n, count), 0) == home_ref[...]
    home_rank = jnp.where(home, dot(home.astype(F32).astype(BF16), earlier), -1.0)
    for r in range(8):
        pick_back[n * r : n * (r + 1), :] = jnp.where(home_rank == float(r), 1.0, 0.0).astype(BF16)
    centres = centres_ref[...]
    tx = targets_ref[0:16, :] - centres[0:1, :]
    ty = targets_ref[16:32, :] - centres[1:2, :]
    tz = targets_ref[32:48, :] - centres[2:3, :]

    def keep(m, l, part, value):
        table[PLACE[(m, l, part)]] = value * weight(l, m)

    harmonics(tx, ty, tz, tx * tx + ty * ty + tz * tz, jnp.ones_like(tx), keep)
    padded = jnp.concatenate([centres, jnp.zeros((5, count), F32)], axis=0)
    centre_parts = jnp.concatenate(
        [part.astype(F32) for part in split3(padded)] + [jnp.zeros((8, count), F32)], axis=0
    ).astype(BF16)
    lanes = jnp.concatenate([up_ref[...]] * 8, axis=0)
    is_density = (iota(lanes.shape, 0) // NODES) % 4 == 3
    lanes = jnp.where(is_density, lanes * fw_ref[...], lanes)
    lanes = jnp.concatenate([lanes, lanes], axis=1).T[0:FINE, :]
    which = (iota(lanes.shape, 1) // NODES) % 4
    up = jnp.concatenate([jnp.where(which == c, lanes, 0.0) for c in range(4)], axis=0)
    up_hi, up_mid, up_lo = split3(up)
    up_a = jnp.concatenate([up_hi, up_hi], axis=1)
    up_b = jnp.concatenate([up_mid, up_mid], axis=1)
    up_c = jnp.concatenate([up_hi, up_lo], axis=1)
    local[...] = jnp.zeros_like(local)
    moments[...] = jnp.zeros_like(moments)
    lane64 = iota((64, 128), 1) < 64
    source_row = (iota((8, 128), 1) // 8) % 8 == iota((8, 128), 0)
    index = iota((count, 128), 0).astype(F32)

    def work(step, carry):
        q = (me // 8 + groups - step) % groups
        pltpu.make_async_copy(
            out_box.at[pl.ds(0, 8)], in_box.at[pl.ds(q * 8, 8)], recv_sem.at[q]
        ).wait()
        rows = in_box[pl.ds(q * 8, 8), 0:8, :].reshape(64, 128)
        rows = jnp.concatenate([jnp.where(lane64, rows, 0.0), jnp.where(lane64, 0.0, rows)], axis=0)
        hi, mid, lo = split3(rows)
        fine = dot(up_a, jnp.concatenate([hi, mid], axis=1), NT)
        fine = fine + dot(up_b, jnp.concatenate([hi, mid], axis=1), NT)
        fine = fine + dot(up_c, jnp.concatenate([lo, hi], axis=1), NT)
        named = in_box[pl.ds(q * 8, 8), 8, :]
        named = jnp.sum(jnp.where(source_row, named, 0.0), axis=0, keepdims=True)
        pick = jnp.where(index == named, 1.0, 0.0).astype(BF16)
        centre = dot(centre_parts, pick)
        centre = centre[0:8, :] + centre[8:16, :] + centre[16:24, :]
        part_rows = 32
        for piece in range(FINE // part_rows):
            at = piece * part_rows
            x = fine[at : at + part_rows, :] - centre[0:1, :]
            y = fine[FINE + at : FINE + at + part_rows, :] - centre[1:2, :]
            z = fine[2 * FINE + at : 2 * FINE + at + part_rows, :] - centre[2:3, :]
            strength = fine[3 * FINE + at : 3 * FINE + at + part_rows, :]
            dist = jnp.maximum(x * x + y * y + z * z, 0.01)
            inverse = 1.0 / dist
            start = strength * jnp.sqrt(inverse)

            def add(m, l, part, value):
                total = value[0:8, :]
                for k in range(1, part_rows // 8):
                    total = total + value[8 * k : 8 * k + 8, :]
                place = PLACE[(m, l, part)] * 8
                if piece:
                    total = total + moments[place : place + 8, :]
                moments[place : place + 8, :] = total

            harmonics(x * inverse, y * inverse, z * inverse, inverse, start, add)
        total = moments[pl.ds(0, ROWS, stride=8), :]
        for k in range(1, 8):
            total = total + moments[pl.ds(k, ROWS, stride=8), :]
        stacked = jnp.concatenate([part.astype(F32) for part in split3(total)], axis=0).astype(BF16)
        local[...] += dot(stacked, pick, NT)
        return carry

    lax.fori_loop(0, groups, work, 0)

    potential = jnp.zeros((NODES, count), F32)
    for place in range(len(PLACE)):
        coefficient = (
            local[place : place + 1, :]
            + local[ROWS + place : ROWS + place + 1, :]
            + local[2 * ROWS + place : 2 * ROWS + place + 1, :]
        )
        potential = potential + table[place] * coefficient
    back = jnp.concatenate([potential] * 8, axis=0)
    back = jnp.concatenate([part.astype(F32) for part in split3(back)], axis=0).astype(BF16)
    lane_slot = iota((n, 128), 1) // NODES
    answer = jnp.zeros((n, 128), F32)
    for r in range(8):
        found = dot(pick_back[n * r : n * (r + 1), :], back, NT)
        found = found[:, 0:128] + found[:, 128:256] + found[:, 256:384]
        answer = jnp.where(lane_slot == r, found, answer)
    back_box[...] = answer.reshape(n, 1, 128)

    def send_back(i, carry):
        p = (me + i) % n
        pltpu.make_async_remote_copy(
            src_ref=back_box.at[p],
            dst_ref=out_ref.at[me],
            send_sem=back_send_sem,
            recv_sem=back_recv_sem,
            device_id=device(p),
            device_id_type=MESH,
        ).start()
        return carry

    lax.fori_loop(1, n, send_back, 0)
    pltpu.make_async_copy(back_box.at[me], out_ref.at[me], back_recv_sem).start()
    pltpu.make_async_copy(
        out_box.at[pl.ds(0, n - 1)], in_box.at[pl.ds(0, n - 1)], send_sem
    ).wait()
    pltpu.make_async_copy(
        back_box.at[pl.ds(0, n - 1)], out_ref.at[pl.ds(0, n - 1)], back_send_sem
    ).wait()
    pltpu.make_async_copy(back_box, out_ref, back_recv_sem).wait()


def per_device(
    grp_size,
    dev_size,
    panel_nodes,
    density,
    crevice_routes,
    crevice_centre,
    centres,
    targets,
    centre_home,
    upsample,
    fine_weights,
):
    n = grp_size * dev_size
    panels = crevice_routes.shape[0]
    count = centres.shape[1]
    pay = jnp.concatenate(
        [
            panel_nodes.reshape(3, panels, NODES).transpose(1, 0, 2).reshape(panels, 3 * NODES),
            density.reshape(panels, NODES),
        ],
        axis=1,
    )
    tall = targets.reshape(3, count, NODES).transpose(0, 2, 1).reshape(3 * NODES, count)
    vmem = pl.BlockSpec(memory_space=pltpu.VMEM)
    returned = pl.pallas_call(
        functools.partial(kernel, grp_size, dev_size),
        out_shape=jax.ShapeDtypeStruct((n, 1, 128), F32),
        in_specs=[vmem] * 8,
        out_specs=vmem,
        scratch_shapes=[
            pltpu.VMEM((n, panels), F32),
            pltpu.VMEM((n, panels), F32),
            pltpu.VMEM((n, 9, 128), F32),
            pltpu.VMEM((n, 9, 128), F32),
            pltpu.VMEM((n, 1, 128), F32),
            pltpu.VMEM((len(PLACE), NODES, count), F32),
            pltpu.VMEM((8 * n, count), BF16),
            pltpu.VMEM((ROWS * 8, 128), F32),
            pltpu.VMEM((3 * ROWS, count), F32),
            pltpu.SemaphoreType.DMA,
            pltpu.SemaphoreType.DMA((n // 8,)),
            pltpu.SemaphoreType.DMA,
            pltpu.SemaphoreType.DMA,
        ],
        compiler_params=pltpu.CompilerParams(
            collective_id=0, has_side_effects=True, vmem_limit_bytes=48 << 20
        ),
    )(
        pay,
        crevice_routes.T,
        crevice_centre.T,
        centre_home.reshape(1, count),
        centres,
        tall,
        upsample.T,
        fine_weights.reshape(1, FINE),
    )
    return returned.reshape(-1)


def solution(mesh):
    split = P(None, ("grp", "dev"))
    rows = P(("grp", "dev"), None)
    placed = (split, P(("grp", "dev")), rows, rows, split, split, rows, P(), P())
    return jax.shard_map(
        functools.partial(per_device, mesh.shape["grp"], mesh.shape["dev"]),
        mesh=mesh,
        in_specs=placed,
        out_specs=P(("grp", "dev")),
        check_vma=False,
    )
```

time: 165 us -> 47 us (0.28)
  local copies, waits for them, and re-layouts: 55 us -> 4.16 us
  other arithmetic: 46.2 us -> 0.14 us
  Pallas kernels: 0 us -> 42.4 us
  waiting for transfers between devices: 26.2 us -> 0 us
  starting transfers between devices: 21.3 us -> 0 us
  blocking collectives: 13.7 us -> 0 us
    pallas_call x0 -> x1, Pallas kernels: none -> 42.4 us  [per_device(): pl.pallas_call(functools.partial(kernel, grp_size, dev_size), out_shape=j...]
    reduce_sum x18 -> x0, other arithmetic: 32.2 us -> none  [the longest x4 17.8 us: expansion_terms(): return jnp.sum(sources[:, 3, :, None] * kernel, axis=1)]
    all_to_all x2 -> x0, waiting for transfers between devices: 26.2 us -> none  [the longest x1 26.2 us: per_device(): lax.all_to_all(outgoing, ('grp', 'dev'), split_axis=0, concat_axis=0, til...]
    all_to_all x2 -> x0, starting transfers between devices: 21.3 us -> none  [the longest x1 11.5 us: per_device(): lax.all_to_all(centre_slot, ('grp', 'dev'), split_axis=0, concat_axis=0,...]
    gather x12 -> x0, local copies, waits for them, and re-layouts: 15.5 us -> none  [the longest x4 10.9 us: one_block(): target_pos = target_all[:, safe_ids, :].transpose(1, 0, 2)]
    scatter x3 -> x0, local copies, waits for them, and re-layouts: 13.8 us -> none  [the longest x1 7.68 us: per_device(): outgoing = jnp.broadcast_to(filler[None, :], (slots, 4 * per_row)).at[slo...]
    all_to_all x1 -> x0, blocking collectives: 13.7 us -> none  [per_device(): lax.all_to_all(sending, ('grp', 'dev'), split_axis=0, concat_axis=0, tile...]
    scatter-add x1 -> x0, other arithmetic: 11.5 us -> none  [per_device(): jax.ops.segment_sum(terms.reshape(slots, nodes), centre_ids, num_segments...]
  transfers between devices with their start and end apart: 2 -> 0, of which waited for: 1 -> 0; matrix products, arithmetic and copies ran while one was open for 10% -> 0% of each run, Pallas kernels for 0% -> 0%
where the time goes in v1:
time: 47 us; the launch traced here: 46.8 us
  Pallas kernels  42.4 us (90%)
  local copies, waits for them, and re-layouts  4.16 us (9%)
    pallas_call x1, Pallas kernels, per_device(): pl.pallas_call(functools.partial(kernel, grp_size, dev_size), out_shape=j...  42.4 us
    unnamed x17, local copies, waits for them, and re-layouts  2.09 us

profile of v1, /device:TPU:1, one launch (start us, length us, event | category | flops | bytes accessed | tf_op | source)
XLA Modules:
  0.0 46.8 jit_solution(7986784466165112105)
XLA Ops:
  0.0 0.0 copy-start.6
  0.0 0.9 %reshape.26 = f32[512,16]{1,0:T(8,128)S(1)} reshape(f32[8192]{0:T(1024)} %param.10) | data formatting | bytes 65536 | tf_op jit(solution)/shard_map/reshape | solution.py:321
  0.9 0.0 copy-done.6
  0.9 0.3 reshape.24
  1.2 0.2 copy.12
  1.5 0.1 copy.13
  1.6 0.0 copy-start.7
  1.6 0.1 pad_maximum_fusion.pay_ref
  1.7 0.8 %copy-done.7 = f32[3,8192]{1,0:T(4,128)S(1)} copy-done((f32[3,8192]{1,0:T(4,128)S(1)}, f32[3,8192]{1,0:T(4,128)}, u32[]{:S(2)}) %copy-start.7) | copy-done | bytes 98328
  2.5 0.3 reshape.28
  2.8 0.0 copy-start
  2.8 0.0 copy-start.1
  2.8 0.0 copy-start.2
  2.8 0.0 copy-start.3
  2.8 0.0 copy-start.4
  2.9 0.2 copy.14
  3.1 0.0 copy-start.5
  3.1 0.4 copy-done
  3.5 0.0 copy-done.1
  3.5 0.0 copy-done.2
  3.5 0.0 copy-done.3
  3.5 0.0 copy-done.4
  3.5 0.2 copy-done.5
  3.8 42.4 %shard_map.91 = f32[128,1,128]{2,1,0:T(1,128)S(1)} custom-call(f32[512,64]{1,0:T(8,128)S(1)} %pad_maximum_fusion.pay_ref, s32[2,512]{1,0:T(2,128)S(1)} %bitcast.13, s32[2,512]{1,0:T(2,128)S(1)} %bitcast.14, s32[1,512]{1,0:T(1,128)S(1)} %bitcast.15, f32[3,512]{1,0:T(4,128)S(1)} %copy-done, f32[48,512]{1,0:T(8,128)S(1)} %bitcast.10, f32[16,64]{1,0:T(8,128)S(1)} %bitcast.12, ...), custom_call_target="tpu_custom_call" | custom-call | tf_op jit(solution)/shard_map/pallas_call | solution.py:327
  46.2 0.6 %copy.16 = f32[16384]{0:T(1024)} copy(f32[16384]{0:T(1024)S(1)} %bitcast.11) | data formatting | bytes 131072
Async XLA Ops:
  0.0 0.9 %copy-start.6 = (f32[3,8192]{1,0:T(4,128)S(1)}, f32[3,8192]{1,0:T(4,128)}, u32[]{:S(2)}) copy-start(f32[3,8192]{1,0:T(4,128)} %param.9) | copy-start | bytes 294916
  1.6 0.9 %copy-start.7 = (f32[3,8192]{1,0:T(4,128)S(1)}, f32[3,8192]{1,0:T(4,128)}, u32[]{:S(2)}) copy-start(f32[3,8192]{1,0:T(4,128)} %param.14) | copy-start | bytes 294916
  2.8 0.7 %copy-start = (f32[3,512]{1,0:T(4,128)S(1)}, f32[3,512]{1,0:T(4,128)}, u32[]{:S(2)}) copy-start(f32[3,512]{1,0:T(4,128)} %centres_ref.1) | copy-start | bytes 18436
  2.8 0.7 %copy-start.1 = (f32[64,16]{0,1:T(8,128)S(1)}, f32[64,16]{0,1:T(8,128)}, u32[]{:S(2)}) copy-start(f32[64,16]{0,1:T(8,128)} %param.16) | copy-start | bytes 12292
  2.8 0.7 %copy-start.2 = (s32[512,2]{0,1:T(2,128)S(1)}, s32[512,2]{0,1:T(2,128)}, u32[]{:S(2)}) copy-start(s32[512,2]{0,1:T(2,128)} %param.11) | copy-start | bytes 12292
  2.8 0.7 %copy-start.3 = (s32[512,2]{0,1:T(2,128)S(1)}, s32[512,2]{0,1:T(2,128)}, u32[]{:S(2)}) copy-start(s32[512,2]{0,1:T(2,128)} %param.12) | copy-start | bytes 12292
  2.8 0.7 %copy-start.4 = (s32[512,1]{0,1:T(1,128)S(1)}, s32[512,1]{0,1:T(1,128)}, u32[]{:S(2)}) copy-start(s32[512,1]{0,1:T(1,128)} %param.15) | copy-start | bytes 6148
  3.1 0.7 %copy-start.5 = (f32[64]{0:T(128)S(1)}, f32[64]{0:T(128)}, u32[]{:S(2)}) copy-start(f32[64]{0:T(128)} %param.17) | copy-start | bytes 772

commit v2 on v1

--- a/solution.py
+++ b/solution.py
@@ -96,7 +96,13 @@
     back_box,
     table,
     pick_back,
-    moments,
+    up_ref2,
+    points_a,
+    points_b,
+    pick_a,
+    pick_b,
+    moments_a,
+    moments_b,
     local,
     send_sem,
     recv_sem,
@@ -202,39 +208,46 @@
     lanes = jnp.concatenate([lanes, lanes], axis=1).T[0:FINE, :]
     which = (iota(lanes.shape, 1) // NODES) % 4
     up = jnp.concatenate([jnp.where(which == c, lanes, 0.0) for c in range(4)], axis=0)
-    up_hi, up_mid, up_lo = split3(up)
-    up_a = jnp.concatenate([up_hi, up_hi], axis=1)
-    up_b = jnp.concatenate([up_mid, up_mid], axis=1)
-    up_c = jnp.concatenate([up_hi, up_lo], axis=1)
+    up_hi, up_mid, _ = split3(up)
+    up_ref2[...] = jnp.concatenate([up_hi, up_hi, up_mid, up_mid], axis=1)
     local[...] = jnp.zeros_like(local)
-    moments[...] = jnp.zeros_like(moments)
+    moments_a[...] = jnp.zeros_like(moments_a)
+    moments_b[...] = jnp.zeros_like(moments_b)
+    pick_b[...] = jnp.zeros_like(pick_b)
     lane64 = iota((64, 128), 1) < 64
     source_row = (iota((8, 128), 1) // 8) % 8 == iota((8, 128), 0)
     index = iota((count, 128), 0).astype(F32)
 
-    def work(step, carry):
+    def prepare(step, points, pick):
         q = (me // 8 + groups - step) % groups
         pltpu.make_async_copy(
             out_box.at[pl.ds(0, 8)], in_box.at[pl.ds(q * 8, 8)], recv_sem.at[q]
         ).wait()
         rows = in_box[pl.ds(q * 8, 8), 0:8, :].reshape(64, 128)
         rows = jnp.concatenate([jnp.where(lane64, rows, 0.0), jnp.where(lane64, 0.0, rows)], axis=0)
-        hi, mid, lo = split3(rows)
-        fine = dot(up_a, jnp.concatenate([hi, mid], axis=1), NT)
-        fine = fine + dot(up_b, jnp.concatenate([hi, mid], axis=1), NT)
-        fine = fine + dot(up_c, jnp.concatenate([lo, hi], axis=1), NT)
+        hi = rows.astype(BF16)
+        mid = (rows - hi.astype(F32)).astype(BF16)
+        both = jnp.concatenate([hi, mid, hi, mid], axis=1)
+        fine = dot(up_ref2[...], both, NT)
         named = in_box[pl.ds(q * 8, 8), 8, :]
         named = jnp.sum(jnp.where(source_row, named, 0.0), axis=0, keepdims=True)
-        pick = jnp.where(index == named, 1.0, 0.0).astype(BF16)
-        centre = dot(centre_parts, pick)
+        picked = jnp.where(index == named, 1.0, 0.0).astype(BF16)
+        centre = dot(centre_parts, picked)
         centre = centre[0:8, :] + centre[8:16, :] + centre[16:24, :]
+        pick[:, 0:128] = picked
+        pick[:, 128:256] = picked
+        for c in range(3):
+            points[c * FINE : (c + 1) * FINE, :] = fine[c * FINE : (c + 1) * FINE, :] - centre[c : c + 1, :]
+        points[3 * FINE : 4 * FINE, :] = fine[3 * FINE : 4 * FINE, :]
+
+    def expand(points, moments):
         part_rows = 32
         for piece in range(FINE // part_rows):
             at = piece * part_rows
-            x = fine[at : at + part_rows, :] - centre[0:1, :]
-            y = fine[FINE + at : FINE + at + part_rows, :] - centre[1:2, :]
-            z = fine[2 * FINE + at : 2 * FINE + at + part_rows, :] - centre[2:3, :]
-            strength = fine[3 * FINE + at : 3 * FINE + at + part_rows, :]
+            x = points[at : at + part_rows, :]
+            y = points[FINE + at : FINE + at + part_rows, :]
+            z = points[2 * FINE + at : 2 * FINE + at + part_rows, :]
+            strength = points[3 * FINE + at : 3 * FINE + at + part_rows, :]
             dist = jnp.maximum(x * x + y * y + z * z, 0.01)
             inverse = 1.0 / dist
             start = strength * jnp.sqrt(inverse)
@@ -249,23 +262,37 @@
                 moments[place : place + 8, :] = total
 
             harmonics(x * inverse, y * inverse, z * inverse, inverse, start, add)
+
+    def gather(moments, pick):
         total = moments[pl.ds(0, ROWS, stride=8), :]
         for k in range(1, 8):
             total = total + moments[pl.ds(k, ROWS, stride=8), :]
-        stacked = jnp.concatenate([part.astype(F32) for part in split3(total)], axis=0).astype(BF16)
-        local[...] += dot(stacked, pick, NT)
+        hi = total.astype(BF16).astype(F32)
+        both = jnp.concatenate([hi, total - hi], axis=1).astype(BF16)
+        local[...] += dot(both, pick[...], NT)
+
+    prepare(0, points_a, pick_a)
+
+    def pair(i, carry):
+        gather(moments_b, pick_b)
+        prepare(2 * i + 1, points_b, pick_b)
+        expand(points_a, moments_a)
+        gather(moments_a, pick_a)
+        prepare(2 * i + 2, points_a, pick_a)
+        expand(points_b, moments_b)
         return carry
 
-    lax.fori_loop(0, groups, work, 0)
+    lax.fori_loop(0, groups // 2 - 1, pair, 0)
+    gather(moments_b, pick_b)
+    prepare(groups - 1, points_b, pick_b)
+    expand(points_a, moments_a)
+    gather(moments_a, pick_a)
+    expand(points_b, moments_b)
+    gather(moments_b, pick_b)
 
     potential = jnp.zeros((NODES, count), F32)
     for place in range(len(PLACE)):
-        coefficient = (
-            local[place : place + 1, :]
-            + local[ROWS + place : ROWS + place + 1, :]
-            + local[2 * ROWS + place : 2 * ROWS + place + 1, :]
-        )
-        potential = potential + table[place] * coefficient
+        potential = potential + table[place] * local[place : place + 1, :]
     back = jnp.concatenate([potential] * 8, axis=0)
     back = jnp.concatenate([part.astype(F32) for part in split3(back)], axis=0).astype(BF16)
     lane_slot = iota((n, 128), 1) // NODES
@@ -337,8 +364,14 @@
             pltpu.VMEM((n, 1, 128), F32),
             pltpu.VMEM((len(PLACE), NODES, count), F32),
             pltpu.VMEM((8 * n, count), BF16),
+            pltpu.VMEM((4 * FINE, 512), BF16),
+            pltpu.VMEM((4 * FINE, 128), F32),
+            pltpu.VMEM((4 * FINE, 128), F32),
+            pltpu.VMEM((count, 256), BF16),
+            pltpu.VMEM((count, 256), BF16),
             pltpu.VMEM((ROWS * 8, 128), F32),
-            pltpu.VMEM((3 * ROWS, count), F32),
+            pltpu.VMEM((ROWS * 8, 128), F32),
+            pltpu.VMEM((ROWS, count), F32),
             pltpu.SemaphoreType.DMA,
             pltpu.SemaphoreType.DMA((n // 8,)),
             pltpu.SemaphoreType.DMA,

time: 47 us -> 43.1 us (0.917)
  Pallas kernels: 42.4 us -> 38.5 us
    pallas_call x1, Pallas kernels: 42.4 us -> 38.5 us  [per_device(): pl.pallas_call(functools.partial(kernel, grp_size, dev_size), out_shape=j...]
where the time goes in v2:
time: 43.1 us; the launch traced here: 42.9 us
  Pallas kernels  38.5 us (89%)
  local copies, waits for them, and re-layouts  4.16 us (10%)
    pallas_call x1, Pallas kernels, per_device(): pl.pallas_call(functools.partial(kernel, grp_size, dev_size), out_shape=j...  38.5 us
    unnamed x17, local copies, waits for them, and re-layouts  2.09 us
    reshape x1, local copies, waits for them, and re-layouts, per_device(): density.reshape(panels, NODES)  0.91 us

profile of v2, /device:TPU:1, one launch (start us, length us, event | category | flops | bytes accessed | tf_op | source)
XLA Modules:
  0.0 42.9 jit_solution(11616784357457765551)
XLA Ops:
  0.0 0.0 copy-start.6
  0.0 0.9 %reshape.26 = f32[512,16]{1,0:T(8,128)S(1)} reshape(f32[8192]{0:T(1024)} %param.10) | data formatting | bytes 65536 | tf_op jit(solution)/shard_map/reshape | solution.py:348
  0.9 0.0 copy-done.6
  0.9 0.3 reshape.24
  1.2 0.2 copy.12
  1.5 0.1 copy.13
  1.6 0.0 copy-start.7
  1.6 0.1 pad_maximum_fusion.pay_ref
  1.7 0.8 %copy-done.7 = f32[3,8192]{1,0:T(4,128)S(1)} copy-done((f32[3,8192]{1,0:T(4,128)S(1)}, f32[3,8192]{1,0:T(4,128)}, u32[]{:S(2)}) %copy-start.7) | copy-done | bytes 98328
  2.5 0.3 reshape.28
  2.8 0.0 copy-start
  2.8 0.0 copy-start.1
  2.8 0.0 copy-start.2
  2.8 0.0 copy-start.3
  2.8 0.0 copy-start.4
  2.9 0.2 copy.14
  3.1 0.0 copy-start.5
  3.1 0.4 copy-done
  3.5 0.0 copy-done.1
  3.5 0.0 copy-done.2
  3.5 0.0 copy-done.3
  3.5 0.0 copy-done.4
  3.5 0.2 copy-done.5
  3.8 38.5 %shard_map.91 = f32[128,1,128]{2,1,0:T(1,128)S(1)} custom-call(f32[512,64]{1,0:T(8,128)S(1)} %pad_maximum_fusion.pay_ref, s32[2,512]{1,0:T(2,128)S(1)} %bitcast.13, s32[2,512]{1,0:T(2,128)S(1)} %bitcast.14, s32[1,512]{1,0:T(1,128)S(1)} %bitcast.15, f32[3,512]{1,0:T(4,128)S(1)} %copy-done, f32[48,512]{1,0:T(8,128)S(1)} %bitcast.10, f32[16,64]{1,0:T(8,128)S(1)} %bitcast.12, ...), custom_call_target="tpu_custom_call" | custom-call | tf_op jit(solution)/shard_map/pallas_call | solution.py:354
  42.2 0.6 %copy.16 = f32[16384]{0:T(1024)} copy(f32[16384]{0:T(1024)S(1)} %bitcast.11) | data formatting | bytes 131072
Async XLA Ops:
  0.0 0.9 %copy-start.6 = (f32[3,8192]{1,0:T(4,128)S(1)}, f32[3,8192]{1,0:T(4,128)}, u32[]{:S(2)}) copy-start(f32[3,8192]{1,0:T(4,128)} %param.9) | copy-start | bytes 294916
  1.6 0.9 %copy-start.7 = (f32[3,8192]{1,0:T(4,128)S(1)}, f32[3,8192]{1,0:T(4,128)}, u32[]{:S(2)}) copy-start(f32[3,8192]{1,0:T(4,128)} %param.14) | copy-start | bytes 294916
  2.8 0.7 %copy-start = (f32[3,512]{1,0:T(4,128)S(1)}, f32[3,512]{1,0:T(4,128)}, u32[]{:S(2)}) copy-start(f32[3,512]{1,0:T(4,128)} %centres_ref.1) | copy-start | bytes 18436
  2.8 0.7 %copy-start.1 = (f32[64,16]{0,1:T(8,128)S(1)}, f32[64,16]{0,1:T(8,128)}, u32[]{:S(2)}) copy-start(f32[64,16]{0,1:T(8,128)} %param.16) | copy-start | bytes 12292
  2.8 0.7 %copy-start.2 = (s32[512,2]{0,1:T(2,128)S(1)}, s32[512,2]{0,1:T(2,128)}, u32[]{:S(2)}) copy-start(s32[512,2]{0,1:T(2,128)} %param.11) | copy-start | bytes 12292
  2.8 0.7 %copy-start.3 = (s32[512,2]{0,1:T(2,128)S(1)}, s32[512,2]{0,1:T(2,128)}, u32[]{:S(2)}) copy-start(s32[512,2]{0,1:T(2,128)} %param.12) | copy-start | bytes 12292
  2.8 0.7 %copy-start.4 = (s32[512,1]{0,1:T(1,128)S(1)}, s32[512,1]{0,1:T(1,128)}, u32[]{:S(2)}) copy-start(s32[512,1]{0,1:T(1,128)} %param.15) | copy-start | bytes 6148
  3.1 0.7 %copy-start.5 = (f32[64]{0:T(128)S(1)}, f32[64]{0:T(128)}, u32[]{:S(2)}) copy-start(f32[64]{0:T(128)} %param.17) | copy-start | bytes 772

commit v3 on v2

--- a/solution.py
+++ b/solution.py
@@ -80,17 +80,21 @@
 def kernel(
     grp_size,
     dev_size,
-    pay_ref,
-    routes_ref,
-    ids_ref,
-    home_ref,
-    centres_ref,
-    targets_ref,
-    up_ref,
-    fw_ref,
+    nodes_hbm,
+    density_hbm,
+    routes_hbm,
+    ids_hbm,
+    home_hbm,
+    centres_hbm,
+    targets_hbm,
+    up_hbm,
+    fw_hbm,
     out_ref,
+    stage,
+    pay_scr,
+    pay_parts,
     rank_scr,
-    value_scr,
+    rank_scr2,
     out_box,
     in_box,
     back_box,
@@ -108,9 +112,37 @@
     recv_sem,
     back_send_sem,
     back_recv_sem,
+    nodes_ref,
+    density_ref,
+    routes_ref,
+    ids_ref,
+    home_ref,
+    centres_ref,
+    targets_ref,
+    up_ref,
+    fw_ref,
+    load_sem,
 ):
     n = grp_size * dev_size
-    panels = pay_ref.shape[0]
+    loads = [
+        pltpu.make_async_copy(source, copy, load_sem.at[i])
+        for i, (source, copy) in enumerate(
+            (
+                (nodes_hbm, nodes_ref),
+                (density_hbm, density_ref),
+                (routes_hbm, routes_ref),
+                (ids_hbm, ids_ref),
+                (home_hbm, home_ref),
+                (centres_hbm, centres_ref),
+                (targets_hbm, targets_ref),
+                (up_hbm, up_ref),
+                (fw_hbm, fw_ref),
+            )
+        )
+    ]
+    for load in loads:
+        load.start()
+    panels = routes_ref.shape[1]
     count = centres_ref.shape[1]
     groups = n // 8
     me = lax.axis_index("grp") * dev_size + lax.axis_index("dev")
@@ -124,44 +156,70 @@
         pl.semaphore_signal(barrier, inc=1, device_id=device((me + i) % n), device_id_type=MESH)
         return carry
 
-    lax.fori_loop(1, n, greet, 0)
-
+    lax.fori_loop(1, n, greet, 0, unroll=True)
+    for load in loads[:4]:
+        load.wait()
+
+    lane = iota((64, 128), 1)
+    for row in range(64):
+        stage[row * 8 : row * 8 + 3, :] = nodes_ref[:, row * 128 : (row + 1) * 128]
+    parts_of = [stage[pl.ds(c, 64, stride=8), :] for c in range(3)] + [density_ref[...]]
+    turned = [[pltpu.roll(v, t * NODES, 1) if t else v for t in range(8)] for v in parts_of]
+    for g in range(8):
+        built = turned[0][(0 - g) % 8]
+        for c in range(1, 8):
+            built = jnp.where(lane // NODES == c, turned[c % 4][(c - g) % 8], built)
+        pay_scr[pl.ds(g, 64, stride=8), :] = built
     owner = iota((n, panels), 0)
     first, second = owner == routes_ref[0:1, :], owner == routes_ref[1:2, :]
     named = first | second
     earlier = (iota((panels, panels), 0) < iota((panels, panels), 1)).astype(F32).astype(BF16)
     rank = dot(named.astype(F32).astype(BF16), earlier)
-    rank_scr[...] = jnp.where(named, rank, -1.0)
+    rank_scr[...] = jnp.where(first, rank, -1.0)
+    rank_scr2[...] = jnp.where(second, rank, -1.0)
     ids = ids_ref[...].astype(F32) - 256.0
-    value_scr[...] = jnp.where(first, ids[0:1, :], jnp.where(second, ids[1:2, :], 0.0))
-    pay = pay_ref[...]
-    parts = jnp.concatenate(split3(jnp.concatenate([pay, pay], axis=1)), axis=1)
-    ones = jnp.ones((panels, 128), BF16)
-    block = 16
+    for block in range(panels // 128):
+        at = block * 128
+        square = jnp.concatenate(
+            [jnp.broadcast_to(ids[r : r + 1, at : at + 128], (64, 128)) for r in range(2)], axis=0
+        ).T
+        hi, mid, lo = split3(pay_scr[at : at + 128, :])
+        left = iota((128, 128), 1) < 64
+        front = jnp.where(left, hi.astype(F32), mid.astype(F32)).astype(BF16)
+        low = lo.astype(F32)
+        pay_parts[at : at + 128, 0:128] = front
+        pay_parts[panels + at : panels + at + 128, 0:128] = front
+        pay_parts[at : at + 128, 128:256] = jnp.where(left, low, pltpu.roll(square, 64, 1)).astype(BF16)
+        pay_parts[panels + at : panels + at + 128, 128:256] = jnp.where(left, low, square).astype(BF16)
+    block = 32
     left = iota((block * 8, 128), 1) < 64
     own_row = iota((block * 8, 128), 1) % 8 == iota((block * 8, 128), 0) % 8
     row8 = iota((8, panels), 0).astype(F32)
 
     def build(step, carry):
         base = step * block
-        low, high, low_id, high_id = [], [], [], []
+        low, high = [], []
         for d in range(block):
             slot = jnp.broadcast_to(rank_scr[pl.ds(base + d, 1), :], (8, panels))
-            value = jnp.broadcast_to(value_scr[pl.ds(base + d, 1), :], (8, panels))
-            is_low, is_high = slot == row8, slot == row8 + 8.0
-            low.append(jnp.where(is_low, 1.0, 0.0))
-            high.append(jnp.where(is_high, 1.0, 0.0))
-            low_id.append(jnp.where(is_low, value, 0.0))
-            high_id.append(jnp.where(is_high, value, 0.0))
-
-        def gather(pieces, what):
-            return dot(jnp.concatenate(pieces, axis=0).astype(BF16), what)
-
-        a, b = gather(low, parts), gather(high, parts)
-        a = a[:, 0:128] + a[:, 128:256] + a[:, 256:384]
-        b = b[:, 0:128] + b[:, 128:256] + b[:, 256:384]
-        out_box[pl.ds(base, block), 0:8, :] = jnp.where(left, a, b).reshape(block, 8, 128)
-        named_id = jnp.where(left, gather(low_id, ones), gather(high_id, ones)) + 256.0
+            slot2 = jnp.broadcast_to(rank_scr2[pl.ds(base + d, 1), :], (8, panels))
+            for rows, offset in ((low, 0.0), (high, 8.0)):
+                rows.append(
+                    jnp.concatenate(
+                        [
+                            jnp.where(slot == row8 + offset, 1.0, 0.0),
+                            jnp.where(slot2 == row8 + offset, 1.0, 0.0),
+                        ],
+                        axis=1,
+                    )
+                )
+        picked = dot(jnp.concatenate(low + high, axis=0).astype(BF16), pay_parts[...])
+        front, rear = picked[:, 0:128], picked[:, 128:256]
+        front = front + pltpu.roll(front, 64, 1)
+        turned = pltpu.roll(rear, 64, 1)
+        half = block * 8
+        rows = jnp.where(left, front[:half] + rear[:half], front[half:] + turned[half:])
+        out_box[pl.ds(base, block), 0:8, :] = rows.reshape(block, 8, 128)
+        named_id = jnp.where(left, turned[:half], rear[half:]) + 256.0
         named_id = jnp.where(own_row, named_id, 0.0).reshape(block, 8, 128)
         out_box[pl.ds(base, block), 8, :] = jnp.sum(named_id, axis=1)
         return carry
@@ -182,17 +240,40 @@
         ).start()
         return carry
 
-    lax.fori_loop(1, n, send, 0)
+    lax.fori_loop(1, n, send, 0, unroll=True)
     pltpu.make_async_copy(out_box.at[me], in_box.at[me], recv_sem.at[me // 8]).start()
 
+    for load in loads[4:]:
+        load.wait()
     home = iota((n, count), 0) == home_ref[...]
     home_rank = jnp.where(home, dot(home.astype(F32).astype(BF16), earlier), -1.0)
     for r in range(8):
         pick_back[n * r : n * (r + 1), :] = jnp.where(home_rank == float(r), 1.0, 0.0).astype(BF16)
     centres = centres_ref[...]
-    tx = targets_ref[0:16, :] - centres[0:1, :]
-    ty = targets_ref[16:32, :] - centres[1:2, :]
-    tz = targets_ref[32:48, :] - centres[2:3, :]
+    for row in range(64):
+        stage[row * 8 : row * 8 + 3, :] = targets_ref[:, row * 128 : (row + 1) * 128]
+    tall = [stage[pl.ds(c, 64, stride=8), :] for c in range(3)]
+    blank = jnp.zeros((64, 128), F32)
+    tall = [
+        jnp.concatenate([tall[0], blank], axis=0).T,
+        jnp.concatenate([blank, tall[1]], axis=0).T,
+        jnp.concatenate([tall[2], blank], axis=0).T,
+    ]
+    tall = [part.astype(F32) for triple in zip(*[split3(v) for v in tall]) for part in triple]
+    tall = jnp.concatenate(
+        [
+            jnp.concatenate([v[g * NODES : (g + 1) * NODES, :] for g in range(8)], axis=1)
+            for v in tall
+        ],
+        axis=0,
+    ).astype(BF16)
+    spread = iota((8 * 128, count), 0)
+    spread = (spread % 64) * 8 + spread // 128 == iota((8 * 128, count), 1)
+    tall = dot(tall, jnp.where(spread, 1.0, 0.0).astype(BF16))
+    tall = tall[0:48, :] + tall[48:96, :] + tall[96:144, :]
+    tx = tall[0:16, :] - centres[0:1, :]
+    ty = tall[16:32, :] - centres[1:2, :]
+    tz = tall[32:48, :] - centres[2:3, :]
 
     def keep(m, l, part, value):
         table[PLACE[(m, l, part)]] = value * weight(l, m)
@@ -315,7 +396,7 @@
         ).start()
         return carry
 
-    lax.fori_loop(1, n, send_back, 0)
+    lax.fori_loop(1, n, send_back, 0, unroll=True)
     pltpu.make_async_copy(back_box.at[me], out_ref.at[me], back_recv_sem).start()
     pltpu.make_async_copy(
         out_box.at[pl.ds(0, n - 1)], in_box.at[pl.ds(0, n - 1)], send_sem
@@ -342,21 +423,16 @@
     n = grp_size * dev_size
     panels = crevice_routes.shape[0]
     count = centres.shape[1]
-    pay = jnp.concatenate(
-        [
-            panel_nodes.reshape(3, panels, NODES).transpose(1, 0, 2).reshape(panels, 3 * NODES),
-            density.reshape(panels, NODES),
-        ],
-        axis=1,
-    )
-    tall = targets.reshape(3, count, NODES).transpose(0, 2, 1).reshape(3 * NODES, count)
     vmem = pl.BlockSpec(memory_space=pltpu.VMEM)
     returned = pl.pallas_call(
         functools.partial(kernel, grp_size, dev_size),
         out_shape=jax.ShapeDtypeStruct((n, 1, 128), F32),
-        in_specs=[vmem] * 8,
+        in_specs=[pl.BlockSpec(memory_space=pltpu.HBM)] * 9,
         out_specs=vmem,
         scratch_shapes=[
+            pltpu.VMEM((512, 128), F32),
+            pltpu.VMEM((panels, 128), F32),
+            pltpu.VMEM((2 * panels, 256), BF16),
             pltpu.VMEM((n, panels), F32),
             pltpu.VMEM((n, panels), F32),
             pltpu.VMEM((n, 9, 128), F32),
@@ -376,17 +452,28 @@
             pltpu.SemaphoreType.DMA((n // 8,)),
             pltpu.SemaphoreType.DMA,
             pltpu.SemaphoreType.DMA,
+            pltpu.VMEM((3, panels * NODES), F32),
+            pltpu.VMEM((panels * NODES // 128, 128), F32),
+            pltpu.VMEM((2, panels), jnp.int32),
+            pltpu.VMEM((2, panels), jnp.int32),
+            pltpu.VMEM((1, count), jnp.int32),
+            pltpu.VMEM((3, count), F32),
+            pltpu.VMEM((3, count * NODES), F32),
+            pltpu.VMEM((NODES, FINE), F32),
+            pltpu.VMEM((1, FINE), F32),
+            pltpu.SemaphoreType.DMA((9,)),
         ],
         compiler_params=pltpu.CompilerParams(
-            collective_id=0, has_side_effects=True, vmem_limit_bytes=48 << 20
+            collective_id=0, has_side_effects=True, vmem_limit_bytes=58 << 20
         ),
     )(
-        pay,
+        panel_nodes,
+        density.reshape(panels * NODES // 128, 128),
         crevice_routes.T,
         crevice_centre.T,
         centre_home.reshape(1, count),
         centres,
-        tall,
+        targets,
         upsample.T,
         fine_weights.reshape(1, FINE),
     )

time: 43.1 us -> 37.4 us (0.87)
  Pallas kernels: 38.5 us -> 35.8 us
  local copies, waits for them, and re-layouts: 4.16 us -> 1.47 us
    pallas_call x1, Pallas kernels: 38.5 us -> 35.8 us  [per_device(): pl.pallas_call(functools.partial(kernel, grp_size, dev_size), out_shape=j...]
    reshape x4 -> x0, local copies, waits for them, and re-layouts: 1.61 us -> none  [the longest x1 0.91 us: per_device(): density.reshape(panels, NODES)]
    unnamed x17 -> x1, local copies, waits for them, and re-layouts: 2.09 us -> 1.47 us
    transpose x2 -> x0, local copies, waits for them, and re-layouts: 0.46 us -> none  [the longest x1 0.23 us: per_device(): panel_nodes.reshape(3, panels, NODES).transpose(1, 0, 2)]
where the time goes in v3:
time: 37.4 us; the launch traced here: 37.3 us
  Pallas kernels  35.8 us (96%)
  local copies, waits for them, and re-layouts  1.47 us (4%)
    pallas_call x1, Pallas kernels, per_device(): pl.pallas_call(functools.partial(kernel, grp_size, dev_size), out_shape=j...  35.8 us
    unnamed x1, local copies, waits for them, and re-layouts  1.47 us

profile of v3, /device:TPU:1, one launch (start us, length us, event | category | flops | bytes accessed | tf_op | source)
XLA Modules:
  0.0 37.3 jit_solution(11741477420100998068)
XLA Ops:
  0.0 35.8 %shard_map.91 = f32[128,1,128]{2,1,0:T(1,128)} custom-call(f32[3,8192]{1,0:T(4,128)} %nodes_hbm.1, f32[64,128]{1,0:T(8,128)} %bitcast.8, s32[2,512]{1,0:T(2,128)} %bitcast.10, s32[2,512]{1,0:T(2,128)} %bitcast.11, s32[1,512]{1,0:T(1,128)} %bitcast.12, f32[3,512]{1,0:T(4,128)} %centres_hbm.1, f32[3,8192]{1,0:T(4,128)} %targets_hbm.1, f32[16,64]{1,0:T(8,128)} %bitcast.9, ...), custom_call_target="tpu_custom_call" | custom-call | tf_op jit(solution)/shard_map/pallas_call | solution.py:427
  35.8 1.5 %copy.11 = f32[16384]{0:T(1024)} copy(f32[16384]{0:T(1024)} %bitcast.7) | data formatting | bytes 131072

commit v4 on v3

--- a/solution.py
+++ b/solution.py
@@ -378,10 +378,10 @@
     back = jnp.concatenate([part.astype(F32) for part in split3(back)], axis=0).astype(BF16)
     lane_slot = iota((n, 128), 1) // NODES
     answer = jnp.zeros((n, 128), F32)
+    found = dot(pick_back[...], back, NT)
+    found = found[:, 0:128] + found[:, 128:256] + found[:, 256:384]
     for r in range(8):
-        found = dot(pick_back[n * r : n * (r + 1), :], back, NT)
-        found = found[:, 0:128] + found[:, 128:256] + found[:, 256:384]
-        answer = jnp.where(lane_slot == r, found, answer)
+        answer = jnp.where(lane_slot == r, found[n * r : n * (r + 1), :], answer)
     back_box[...] = answer.reshape(n, 1, 128)
 
     def send_back(i, carry):
@@ -426,7 +426,7 @@
     vmem = pl.BlockSpec(memory_space=pltpu.VMEM)
     returned = pl.pallas_call(
         functools.partial(kernel, grp_size, dev_size),
-        out_shape=jax.ShapeDtypeStruct((n, 1, 128), F32),
+        out_shape=pltpu.VMEM((n, 1, 128), F32),
         in_specs=[pl.BlockSpec(memory_space=pltpu.HBM)] * 9,
         out_specs=vmem,
         scratch_shapes=[

time: 37.4 us -> 35.6 us (0.952)
  Pallas kernels: 35.8 us -> 34.8 us
  local copies, waits for them, and re-layouts: 1.47 us -> 0.63 us
    pallas_call x1, Pallas kernels: 35.8 us -> 34.8 us  [per_device(): pl.pallas_call(functools.partial(kernel, grp_size, dev_size), out_shape=p...]
    unnamed x1, local copies, waits for them, and re-layouts: 1.47 us -> 0.63 us
where the time goes in v4:
time: 35.6 us; the launch traced here: 35.5 us
  Pallas kernels  34.8 us (98%)
  local copies, waits for them, and re-layouts  0.63 us (2%)
    pallas_call x1, Pallas kernels, per_device(): pl.pallas_call(functools.partial(kernel, grp_size, dev_size), out_shape=p...  34.8 us

profile of v4, /device:TPU:1, one launch (start us, length us, event | category | flops | bytes accessed | tf_op | source)
XLA Modules:
  0.0 35.5 jit_solution(9608240181017837186)
XLA Ops:
  0.0 34.8 %shard_map.91 = f32[128,1,128]{2,1,0:T(1,128)S(1)} custom-call(f32[3,8192]{1,0:T(4,128)} %nodes_hbm.1, f32[64,128]{1,0:T(8,128)} %bitcast.8, s32[2,512]{1,0:T(2,128)} %bitcast.10, s32[2,512]{1,0:T(2,128)} %bitcast.11, s32[1,512]{1,0:T(1,128)} %bitcast.12, f32[3,512]{1,0:T(4,128)} %centres_hbm.1, f32[3,8192]{1,0:T(4,128)} %targets_hbm.1, f32[16,64]{1,0:T(8,128)} %bitcast.9, ...), custom_call_target="tpu_custom_call" | custom-call | tf_op jit(solution)/shard_map/pallas_call | solution.py:427
  34.9 0.6 %copy.11 = f32[16384]{0:T(1024)} copy(f32[16384]{0:T(1024)S(1)} %bitcast.7) | data formatting | bytes 131072

commit v5 on v4

--- a/solution.py
+++ b/solution.py
@@ -228,20 +228,29 @@
 
     pl.semaphore_wait(barrier, n - 1)
 
-    def send(i, carry):
-        p = (me + i) % n
+    grp, place = lax.axis_index("grp"), lax.axis_index("dev")
+    berth = (place % 8) * groups + me // 8
+    wide = dev_size // 8
+
+    def peer(i):
+        stage, k = i // groups, i % groups
+        column = (grp ^ (k // wide)) * dev_size + (place // 8 + k % wide) % wide * 8
+        return column + ((place % 8) ^ stage)
+
+    def send(i):
+        p = peer(i)
         pltpu.make_async_remote_copy(
             src_ref=out_box.at[p],
-            dst_ref=in_box.at[me],
+            dst_ref=in_box.at[berth],
             send_sem=send_sem,
-            recv_sem=recv_sem.at[me // 8],
+            recv_sem=recv_sem.at[berth // 8],
             device_id=device(p),
             device_id_type=MESH,
         ).start()
-        return carry
-
-    lax.fori_loop(1, n, send, 0, unroll=True)
-    pltpu.make_async_copy(out_box.at[me], in_box.at[me], recv_sem.at[me // 8]).start()
+
+    for i in range(1, n):
+        send(i)
+    pltpu.make_async_copy(out_box.at[me], in_box.at[berth], recv_sem.at[berth // 8]).start()
 
     for load in loads[4:]:
         load.wait()
@@ -300,7 +309,7 @@
     index = iota((count, 128), 0).astype(F32)
 
     def prepare(step, points, pick):
-        q = (me // 8 + groups - step) % groups
+        q = ((place % 8) ^ (step // 2)) * 2 + ((grp // (grp_size // 2)) ^ (step % 2))
         pltpu.make_async_copy(
             out_box.at[pl.ds(0, 8)], in_box.at[pl.ds(q * 8, 8)], recv_sem.at[q]
         ).wait()

time: 35.6 us -> 34.5 us (0.969)
  Pallas kernels: 34.8 us -> 33.8 us
    pallas_call x1, Pallas kernels: 34.8 us -> 33.8 us  [per_device(): pl.pallas_call(functools.partial(kernel, grp_size, dev_size), out_shape=p...]
where the time goes in v5:
time: 34.5 us; the launch traced here: 34.4 us
  Pallas kernels  33.8 us (98%)
  local copies, waits for them, and re-layouts  0.63 us (2%)
    pallas_call x1, Pallas kernels, per_device(): pl.pallas_call(functools.partial(kernel, grp_size, dev_size), out_shape=p...  33.8 us

profile of v5, /device:TPU:1, one launch (start us, length us, event | category | flops | bytes accessed | tf_op | source)
XLA Modules:
  0.0 34.4 jit_solution(9691127116190572902)
XLA Ops:
  0.0 33.8 %shard_map.91 = f32[128,1,128]{2,1,0:T(1,128)S(1)} custom-call(f32[3,8192]{1,0:T(4,128)} %nodes_hbm.1, f32[64,128]{1,0:T(8,128)} %bitcast.8, s32[2,512]{1,0:T(2,128)} %bitcast.10, s32[2,512]{1,0:T(2,128)} %bitcast.11, s32[1,512]{1,0:T(1,128)} %bitcast.12, f32[3,512]{1,0:T(4,128)} %centres_hbm.1, f32[3,8192]{1,0:T(4,128)} %targets_hbm.1, f32[16,64]{1,0:T(8,128)} %bitcast.9, ...), custom_call_target="tpu_custom_call" | custom-call | tf_op jit(solution)/shard_map/pallas_call | solution.py:436
  33.8 0.6 %copy.11 = f32[16384]{0:T(1024)} copy(f32[16384]{0:T(1024)S(1)} %bitcast.7) | data formatting | bytes 131072

commit v6 on v5

--- a/solution.py
+++ b/solution.py
@@ -224,7 +224,7 @@
         out_box[pl.ds(base, block), 8, :] = jnp.sum(named_id, axis=1)
         return carry
 
-    lax.fori_loop(0, n // block, build, 0)
+    lax.fori_loop(0, n // block, build, 0, unroll=2)
 
     pl.semaphore_wait(barrier, n - 1)
 

time: 34.5 us -> 34.2 us (level)
  no operation moved by 1% of the time
where the time goes in v6:
time: 34.2 us; the launch traced here: 34.1 us
  Pallas kernels  33.5 us (98%)
  local copies, waits for them, and re-layouts  0.63 us (2%)
    pallas_call x1, Pallas kernels, per_device(): pl.pallas_call(functools.partial(kernel, grp_size, dev_size), out_shape=p...  33.5 us

profile of v6, /device:TPU:1, one launch (start us, length us, event | category | flops | bytes accessed | tf_op | source)
XLA Modules:
  0.0 34.1 jit_solution(15383671500402802173)
XLA Ops:
  0.0 33.5 %shard_map.91 = f32[128,1,128]{2,1,0:T(1,128)S(1)} custom-call(f32[3,8192]{1,0:T(4,128)} %nodes_hbm.1, f32[64,128]{1,0:T(8,128)} %bitcast.8, s32[2,512]{1,0:T(2,128)} %bitcast.10, s32[2,512]{1,0:T(2,128)} %bitcast.11, s32[1,512]{1,0:T(1,128)} %bitcast.12, f32[3,512]{1,0:T(4,128)} %centres_hbm.1, f32[3,8192]{1,0:T(4,128)} %targets_hbm.1, f32[16,64]{1,0:T(8,128)} %bitcast.9, ...), custom_call_target="tpu_custom_call" | custom-call | tf_op jit(solution)/shard_map/pallas_call | solution.py:436
  33.5 0.6 %copy.11 = f32[16384]{0:T(1024)} copy(f32[16384]{0:T(1024)S(1)} %bitcast.7) | data formatting | bytes 131072
